TPU v7x, 32 devices: a whole 2x2x4 slice. The times are simulated.
32 devices in a mesh: grp: 2 (over y), gx: 4 (over z), gy: 2 (over x), gz: 2 (over core).
Axes of the slice: x: 2, y: 2, z: 4, core: 2. Of those that a mesh axis runs over, the one named last changes fastest.
Arguments:
- parcel_values: bfloat16 [6, 131072], P(None, ('grp', 'gx', 'gy', 'gz')), parts along dimension 1, may hold values from -2304 to 2304
- parcel_owner: int32 [131072, 1], P(('grp', 'gx', 'gy', 'gz')), parts along dimension 0, may hold values from 0 to 3; in each aligned block of 4096 rows (0 to 4095, 4096 to 8191, ...) at most 1536 rows name the same one
- parcel_cell: int32 [131072], P(('grp', 'gx', 'gy', 'gz')), parts along dimension 0, may hold values from 0 to 65535
- live_counts: int32 [32], P(('grp', 'gx', 'gy', 'gz')), parts along dimension 0, may hold values from 1 to 4096, 49152 in all
- fluid_state: bfloat16 [6, 256, 32, 256], P(None, ('grp', 'gx'), 'gy', 'gz'), parts along dimension 1, may hold values from -6 to 6
Outputs:
- coupled: bfloat16 [6, 256, 32, 256], P(None, ('grp', 'gx'), 'gy', 'gz'), parts along dimension 1
There are 2 independent parts, one for each index of `grp`. A program takes and returns all parts, laid end to end along the dimension named above; each array names one. Nothing has to cross between parts.
Inputs may be any that keep to these rules, and one draw needn't show every extreme that they name: `parcel_owner`: among the rows of one brick no streamwise index is named by more than 1536 rows; some brick names one exactly 1536 times. `parcel_cell`: cells are numbered (x * 16 + y) * 128 + z within the brick. `live_counts`: A brick's live parcels are its first rows; some brick has all rows live.
All inputs are finite; a program needn't handle non-finite values. No bound on the sum of `live_counts` on one device may be relied on, other than what follows from the above.
Results may differ from a plain program's by a relative error of at most 0.005.
Values may be sent and summed in bfloat16 or wider, within the bound.
A program may use at most 64 MiB of HBM per device.

v0:
```python
import jax
import jax.numpy as jnp
from jax import lax
from jax.sharding import PartitionSpec as P

REACH = 16
spread_cells = 12.0


def padded(shard, sides, width):
    for axis, dim in sides:
        size, length = (lax.axis_size(axis), shard.shape[dim])
        up = [(i, (i + 1) % size) for i in range(size)]
        down = [(j, i) for i, j in up]
        last = lax.slice_in_dim(shard, length - width, length, axis=dim)
        initial = lax.slice_in_dim(shard, 0, width, axis=dim)
        before = lax.ppermute(last, axis, up)
        after = lax.ppermute(initial, axis, down)
        shard = jnp.concatenate([before, shard, after], axis=dim)
    return shard


def tap_curve(offsets):
    tap_grid = jnp.arange(2 * REACH + 1).astype(jnp.float32)
    tap_sum = jnp.sum(
        jnp.exp(-(tap_grid - REACH) * (tap_grid - REACH) / (2.0 * spread_cells * spread_cells))
    )
    return (
        jnp.exp(-(offsets - REACH) * (offsets - REACH) / (2.0 * spread_cells * spread_cells))
        / tap_sum
    )


def banded(out_rows, in_rows, shift):
    row_ids = lax.broadcasted_iota(jnp.int32, (out_rows, in_rows), 0)
    col_ids = lax.broadcasted_iota(jnp.int32, (out_rows, in_rows), 1)
    offset_ids = col_ids - row_ids + shift
    inside = (offset_ids >= 0) & (offset_ids <= 2 * REACH)
    values = tap_curve(offset_ids.astype(jnp.float32)).astype(jnp.bfloat16)
    return jnp.where(inside, values, jnp.zeros_like(values))


def on_device(parcel_values, parcel_owner, parcel_cell, live_counts, fluid_state):
    channels, count_dev = parcel_values.shape
    width_x, width_y, width_z = (fluid_state.shape[1], fluid_state.shape[2], fluid_state.shape[3])
    owners = lax.axis_size("gx")
    capacity = 3 * count_dev // (2 * owners)
    owner_ids = parcel_owner[:, 0]
    local_rows = jnp.arange(count_dev, dtype=jnp.int32)
    is_live = local_rows < live_counts[0]
    owner_hits = (
        (owner_ids[:, None] == jnp.arange(owners, dtype=jnp.int32)[None, :]) & is_live[:, None]
    ).astype(jnp.int32)
    position = jnp.sum(jnp.cumsum(owner_hits, axis=0) * owner_hits, axis=1) - 1
    slot_index = jnp.where(is_live, owner_ids * capacity + position, owners * capacity)
    cell_xpart = (parcel_cell // (width_y * width_z)).astype(jnp.bfloat16)
    cell_ypart = (parcel_cell // width_z % width_y).astype(jnp.bfloat16)
    cell_low = (parcel_cell % width_z).astype(jnp.bfloat16)
    send_rows = jnp.concatenate(
        [parcel_values, cell_xpart[None, :], cell_ypart[None, :], cell_low[None, :]], axis=0
    )
    packed = (
        jnp.zeros((channels + 3, owners * capacity), jnp.bfloat16)
        .at[:, slot_index]
        .set(send_rows, mode="drop")
    )
    packed = packed.reshape(channels + 3, owners, capacity)
    arrived = lax.all_to_all(packed, "gx", split_axis=1, concat_axis=1, tiled=True).reshape(
        channels + 3, owners * capacity
    )
    slot_total = owners * capacity
    block_rows = min(1024, slot_total)
    plane_cells = width_x * width_y
    high_grid = jnp.arange(plane_cells, dtype=jnp.float32)
    low_grid = jnp.arange(width_z, dtype=jnp.float32)

    def deposit(step_index, summed):
        window = lax.dynamic_slice_in_dim(arrived, step_index * block_rows, block_rows, 1)
        high_ids = window[channels].astype(jnp.float32) * width_y + window[channels + 1].astype(
            jnp.float32
        )
        high_hot = (high_ids[:, None] == high_grid[None, :]).astype(jnp.bfloat16)
        low_hot = (window[channels + 2].astype(jnp.float32)[:, None] == low_grid[None, :]).astype(
            jnp.bfloat16
        )
        weighted = window[:channels][:, :, None] * low_hot[None, :, :]
        return summed + jnp.einsum(
            "sh,csz->chz", high_hot, weighted, preferred_element_type=jnp.float32
        )

    summed = lax.fori_loop(
        0,
        slot_total // block_rows,
        deposit,
        jnp.zeros((channels, plane_cells, width_z), jnp.float32),
    )
    source = summed.reshape(channels, width_x, width_y, width_z).astype(jnp.bfloat16)
    flat_source = source.reshape(channels, width_x, width_y * width_z)
    pencil = lax.all_to_all(flat_source, "gx", split_axis=2, concat_axis=1, tiled=True)
    full_x = pencil.shape[1]
    smoothed = jnp.einsum(
        "ij,cjk->cik", banded(full_x, full_x, REACH), pencil, preferred_element_type=jnp.float32
    ).astype(jnp.bfloat16)
    after_x = lax.all_to_all(smoothed, "gx", split_axis=1, concat_axis=2, tiled=True)
    after_x = after_x.reshape(channels, width_x, width_y, width_z)
    extended_y = padded(after_x, (("gy", 2),), REACH)
    after_y = jnp.einsum(
        "ij,cxjz->cxiz",
        banded(width_y, width_y + 2 * REACH, 0),
        extended_y,
        preferred_element_type=jnp.float32,
    ).astype(jnp.bfloat16)
    extended_z = padded(after_y, (("gz", 3),), REACH)
    smooth_z = jnp.einsum(
        "cxyj,ij->cxyi",
        extended_z,
        banded(width_z, width_z + 2 * REACH, 0),
        preferred_element_type=jnp.float32,
    )
    return (fluid_state.astype(jnp.float32) + smooth_z).astype(jnp.bfloat16)


def solution(mesh):
    in_specs = (
        P(None, ("grp", "gx", "gy", "gz")),
        P(("grp", "gx", "gy", "gz"), None),
        P(("grp", "gx", "gy", "gz")),
        P(("grp", "gx", "gy", "gz")),
        P(None, ("grp", "gx"), "gy", "gz"),
    )
    out_specs = P(None, ("grp", "gx"), "gy", "gz")
    return jax.shard_map(
        on_device, mesh=mesh, in_specs=in_specs, out_specs=out_specs, check_vma=False
    )
```

profile of v0, /device:TPU:0, one launch (start us, length us, event | category | flops | bytes accessed | tf_op | source)
XLA Modules:
  0.0 157.6 jit_solution(1705467644931148753)
XLA Ops:
  0.7 0.7 fusion.61
  1.4 1.2 reduce-window.6
  2.6 0.2 slice_reduce_fusion
  2.8 0.2 reduce-window.9
  3.0 0.1 add_bitcast_fusion
  3.1 0.8 fusion.53
  3.9 0.8 fusion.79
  4.8 0.9 maximum_bitcast_fusion
  5.7 0.5 copy.30
  6.3 11.4 %scatter_custom_fusion = bf16[9,6144]{0,1:T(8,128)(2,1)S(1)} fusion(s32[4096]{0:T(1024)S(1)} %bitcast.85, bf16[4096,9]{1,0:T(8,128)(2,1)S(1)} %copy.30, bf16[]{:T(256)} %constant.117.clone.1), kind=kCustom, calls=%fused_computation.36 | custom fusion | bytes 110594 | tf_op jit(solution)/shard_map/scatter | solution.py:65
  17.6 1.4 copy.31
  19.0 6.3 %all-to-all-start = ((bf16[9,4,1536]{2,0,1:T(8,128)(2,1)}), bf16[9,4,1536]{2,0,1:T(8,128)(2,1)S(1)}, u32[]{:S(2)}, u32[]{:S(2)}) async-start(bf16[9,4,1536]{2,0,1:T(8,128)(2,1)} %copy.31), calls=%async_computation | async-start | bytes 393216 | tf_op jit(solution)/shard_map/all_to_all | solution.py:68
  25.3 7.5 %all-to-all-done = bf16[9,4,1536]{2,0,1:T(8,128)(2,1)S(1)} async-done(((bf16[9,4,1536]{2,0,1:T(8,128)(2,1)}), bf16[9,4,1536]{2,0,1:T(8,128)(2,1)S(1)}, u32[]{:S(2)}, u32[]{:S(2)}) %all-to-all-start) | async-done | bytes 110624 | tf_op jit(solution)/shard_map/all_to_all | solution.py:68
  32.8 0.1 copy.32
  32.9 0.1 pad.10
  33.1 9.3 %while.14 = (s32[]{:T(128)}, f32[6,512,128]{1,2,0:T(8,128)S(1)}, bf16[9,6144]{1,0:T(8,128)(2,1)S(1)}, s32[]{:T(128)}, s32[]{:T(128)}, /*index=5*/s32[]{}, s32[]{:T(128)}, s32[]{:T(128)}, s32[]{}, s32[]{}) while((s32[]{:T(128)}, f32[6,512,128]{1,2,0:T(8,128)S(1)}, bf16[9,6144]{1,0:T(8,128)(2,1)S(1)}, s32[]{:T(128)}, s32[]{:T(128)}, ...), condition=%wide.region_5.6_spmd.clone, body=%wide.region_4.5_spmd.clone.sunk | while | flops 807670784 | bytes 3729625 | solution.py:91
  33.1 0.1 fusion.132
  33.2 0.1 fusion.131
  33.3 1.3 bitcast_add_fusion.2
  34.6 0.1 fusion.132
  34.7 0.1 fusion.131
  34.8 1.3 bitcast_add_fusion.2
  36.2 0.1 fusion.132
  36.3 0.1 fusion.131
  36.4 1.3 bitcast_add_fusion.2
  37.7 0.1 fusion.132
  37.8 0.1 fusion.131
  37.9 1.3 bitcast_add_fusion.2
  39.3 0.1 fusion.132
  39.4 0.1 fusion.131
  39.5 1.3 bitcast_add_fusion.2
  40.8 0.1 fusion.132
  40.9 0.1 fusion.131
  41.0 1.3 bitcast_add_fusion.2
  42.4 0.1 convert_element_type.119
  42.5 0.4 copy.33
  42.8 0.3 convert_element_type.120
  43.2 4.2 %copy.34 = bf16[6,32,2048]{1,0,2:T(8,128)(2,1)} copy(bf16[6,32,2048]{2,1,0:T(8,128)(2,1)S(1)} %convert_element_type.120) | data formatting | bytes 1572864 | tf_op jit(solution)/shard_map/convert_element_type | solution.py:97
  47.4 5.7 %reshape.138 = bf16[4,2,49152]{2,1,0:T(2,128)(2,1)} reshape(bf16[2048,6,32]{2,1,0:T(8,128)(2,1)} %bitcast.72) | data formatting | bytes 1572864
  53.1 3.5 %all-to-all-start.1 = ((bf16[4,2,49152]{2,1,0:T(2,128)(2,1)}), bf16[4,2,49152]{2,1,0:T(2,128)(2,1)S(1)}, u32[]{:S(2)}, u32[]{:S(2)}) async-start(bf16[4,2,49152]{2,1,0:T(2,128)(2,1)} %reshape.138), calls=%async_computation.1 | async-start | bytes 1572864 | tf_op jit(solution)/shard_map/all_to_all | solution.py:99
  56.6 0.6 fusion.104
  57.2 18.1 %all-to-all-done.1 = bf16[4,2,49152]{2,1,0:T(2,128)(2,1)S(1)} async-done(((bf16[4,2,49152]{2,1,0:T(2,128)(2,1)}), bf16[4,2,49152]{2,1,0:T(2,128)(2,1)S(1)}, u32[]{:S(2)}, u32[]{:S(2)}) %all-to-all-start.1) | async-done | bytes 786464 | tf_op jit(solution)/shard_map/all_to_all | solution.py:99
  75.3 4.2 %reshape.139 = bf16[2048,6,32]{2,1,0:T(8,128)(2,1)} reshape(bf16[4,2,49152]{2,1,0:T(2,128)(2,1)S(1)} %all-to-all-done.1) | data formatting | bytes 1572864
  79.5 4.5 %copy.48 = bf16[6,32,4,512]{3,2,1,0:T(4,128)(2,1)S(1)} copy(bf16[6,32,4,512]{1,0,3,2:T(8,128)(2,1)} %bitcast.73) | data formatting | bytes 1572864 | tf_op jit(solution)/shard_map/all_to_all | solution.py:99
  84.0 0.2 copy.36
  84.2 1.0 fusion.38
  85.2 0.9 copy.38
  86.1 27.7 %all_to_all.38 = bf16[6,128,512]{2,0,1:T(8,128)(2,1)S(1)} all-to-all(bf16[6,128,512]{2,0,1:T(8,128)(2,1)S(1)} %copy.38), channel_id=1, replica_groups=mesh['grp'=2,'gx'=4,'gy'=2,'gz'=2] {'gx'}, dimensions={1} | all-to-all | bytes 1572864 | tf_op jit(solution)/shard_map/all_to_all | solution.py:104
  113.8 0.6 copy.40
  114.4 0.3 reshape.120
  114.7 1.6 collective-permute-start
  116.2 0.5 collective-permute-start.1
  116.8 18.5 %collective-permute-done = bf16[6,32,16,128]{3,2,1,0:T(8,128)(2,1)S(1)} collective-permute-done((bf16[6,32,16,128]{3,2,1,0:T(8,128)(2,1)S(1)}, bf16[6,32,16,128]{3,2,1,0:T(8,128)(2,1)S(1)}, u32[]{:S(2)}, u32[]{:S(2)}) %collective-permute-start) | collective-permute-done | bytes 786464 | tf_op jit(solution)/shard_map/ppermute | solution.py:17
  135.2 14.4 %collective-permute-done.1 = bf16[6,32,16,128]{3,2,1,0:T(8,128)(2,1)S(1)} collective-permute-done((bf16[6,32,16,128]{3,2,1,0:T(8,128)(2,1)S(1)}, bf16[6,32,16,128]{3,2,1,0:T(8,128)(2,1)S(1)}, u32[]{:S(2)}, u32[]{:S(2)}) %collective-permute-start.1) | collective-permute-done | bytes 786464 | tf_op jit(solution)/shard_map/ppermute | solution.py:18
  149.7 1.1 fusion.35
  150.7 0.4 fusion.123
  151.1 0.6 copy.41
  151.8 0.6 copy.42
  152.5 0.5 collective-permute-start.3
  153.0 0.5 collective-permute-done.2
  153.5 0.6 copy.43
  154.2 0.2 collective-permute-done.3
  154.3 0.6 copy.44
  155.0 2.6 %add_convert_fusion = bf16[6,32,16,128]{3,2,1,0:T(8,128)(2,1)} fusion(bf16[6,32,16,128]{3,2,1,0:T(8,128)(2,1)S(1)} %copy-done.1, bf16[6,32,16,16]{3,2,1,0:T(8,128)(2,1)S(1)} %copy.44, bf16[6,32,16,128]{3,2,1,0:T(8,128)(2,1)S(1)} %fusion.35, bf16[6,32,16,16]{3,2,1,0:T(8,128)(2,1)S(1)} %copy.43, f32[]{:T(128)} %fusion.104), kind=kOutput, calls=%fused_computation.31 | convolution fusion | flops 130203648 | bytes 2555908 | tf_op jit(solution)/shard_map/cxyj,ij->cxyi/dot_general | solution.py:114
  (26 shorter events, 0.3 us)
Async XLA Ops:
  0.0 6.2 %copy-start = (s32[4096,1]{0,1:T(1,128)S(1)}, s32[4096,1]{0,1:T(1,128)}, u32[]{:S(2)}) copy-start(s32[4096,1]{0,1:T(1,128)} %param.8) | copy-start | bytes 49156
  19.0 13.8 %all-to-all-start = ((bf16[9,4,1536]{2,0,1:T(8,128)(2,1)}), bf16[9,4,1536]{2,0,1:T(8,128)(2,1)S(1)}, u32[]{:S(2)}, u32[]{:S(2)}) async-start(bf16[9,4,1536]{2,0,1:T(8,128)(2,1)} %copy.31), calls=%async_computation | async-start | bytes 393216 | tf_op jit(solution)/shard_map/all_to_all | solution.py:68
  53.1 22.2 %all-to-all-start.1 = ((bf16[4,2,49152]{2,1,0:T(2,128)(2,1)}), bf16[4,2,49152]{2,1,0:T(2,128)(2,1)S(1)}, u32[]{:S(2)}, u32[]{:S(2)}) async-start(bf16[4,2,49152]{2,1,0:T(2,128)(2,1)} %reshape.138), calls=%async_computation.1 | async-start | bytes 1572864 | tf_op jit(solution)/shard_map/all_to_all | solution.py:99
  114.7 20.5 %collective-permute-start = (bf16[6,32,16,128]{3,2,1,0:T(8,128)(2,1)S(1)}, bf16[6,32,16,128]{3,2,1,0:T(8,128)(2,1)S(1)}, u32[]{:S(2)}, u32[]{:S(2)}) collective-permute-start(bf16[6,32,16,128]{3,2,1,0:T(8,128)(2,1)S(1)} %reshape.120), channel_id=1, source_target_pairs={{0,2},{2,0},{1,3},{3,1},{4,6},{6,4},{5,7},{7,5},{8,10},{10,8},{9,1... | collective-permute-start | bytes 2359304 | tf_op jit(solution)/shard_map/ppermute | solution.py:17
  116.2 33.4 %collective-permute-start.1 = (bf16[6,32,16,128]{3,2,1,0:T(8,128)(2,1)S(1)}, bf16[6,32,16,128]{3,2,1,0:T(8,128)(2,1)S(1)}, u32[]{:S(2)}, u32[]{:S(2)}) collective-permute-start(bf16[6,32,16,128]{3,2,1,0:T(8,128)(2,1)S(1)} %reshape.120), channel_id=1, source_target_pairs={{2,0},{0,2},{3,1},{1,3},{6,4},{4,6},{7,5},{5,7},{10,8},{8,10},{11,... | collective-permute-start | bytes 2359304 | tf_op jit(solution)/shard_map/ppermute | solution.py:18
  151.7 1.8 %collective-permute-start.2 = (bf16[6,32,16,16]{1,3,2,0:T(8,128)(2,1)S(1)}, bf16[6,32,16,16]{1,3,2,0:T(8,128)(2,1)S(1)}, u32[]{:S(2)}, u32[]{:S(2)}) collective-permute-start(bf16[6,32,16,16]{1,3,2,0:T(8,128)(2,1)S(1)} %copy.41), channel_id=1, source_target_pairs={{0,1},{1,0},{2,3},{3,2},{4,5},{5,4},{6,7},{7,6},{8,9},{9,8},{10,11... | collective-permute-start | bytes 294920 | tf_op jit(solution)/shard_map/ppermute | solution.py:17
  151.8 3.2 %copy-start.1 = (bf16[6,32,16,128]{3,2,1,0:T(8,128)(2,1)S(1)}, bf16[6,32,16,128]{3,2,1,0:T(8,128)(2,1)}, u32[]{:S(2)}) copy-start(bf16[6,32,16,128]{3,2,1,0:T(8,128)(2,1)} %param.11) | copy-start | bytes 2359300
  152.5 1.9 %collective-permute-start.3 = (bf16[6,32,16,16]{1,3,2,0:T(8,128)(2,1)S(1)}, bf16[6,32,16,16]{1,3,2,0:T(8,128)(2,1)S(1)}, u32[]{:S(2)}, u32[]{:S(2)}) collective-permute-start(bf16[6,32,16,16]{1,3,2,0:T(8,128)(2,1)S(1)} %copy.42), channel_id=1, source_target_pairs={{1,0},{0,1},{3,2},{2,3},{5,4},{4,5},{7,6},{6,7},{9,8},{8,9},{11,10... | collective-permute-start | bytes 294920 | tf_op jit(solution)/shard_map/ppermute | solution.py:18
where the time goes:
time: 158 us
  waiting for transfers between devices  59.2 us (37%)
  local copies, waits for them, and re-layouts  37.9 us (24%)
  blocking collectives  27.7 us (18%)
  matrix products  12.6 us (8%)
  starting transfers between devices  12.5 us (8%)
  other arithmetic  6.49 us (4%)
    all_to_all x1, blocking collectives, on_device(): lax.all_to_all(smoothed, 'gx', split_axis=1, concat_axis=2, tiled=True)  27.7 us
    ppermute x2, waiting for transfers between devices, padded(): before = lax.ppermute(last, axis, up)  19 us
    all_to_all x1, waiting for transfers between devices, on_device(): lax.all_to_all(flat_source, 'gx', split_axis=2, concat_axis=1, tiled=True)  18.1 us
    ppermute x2, waiting for transfers between devices, padded(): after = lax.ppermute(initial, axis, down)  14.6 us
    scatter x1, local copies, waits for them, and re-layouts, on_device(): packed = jnp.zeros((channels + 3, owners * capacity), jnp.bfloat16).at[:,...  11.4 us
    unnamed x8, local copies, waits for them, and re-layouts  9.98 us
    dot_general x6, matrix products, deposit(): jnp.einsum('sh,csz->chz', high_hot, weighted, preferred_element_type=jnp....  7.91 us
    all_to_all x1, waiting for transfers between devices, on_device(): lax.all_to_all(packed, 'gx', split_axis=1, concat_axis=1, tiled=True)  7.51 us
  transfers between devices with their start and end apart: 6, of which 6 were waited for; matrix products, arithmetic and copies ran while one was open for 1% of the time, Pallas kernels for 0%

commit v1 on v0

--- a/solution.py
+++ b/solution.py
@@ -41,6 +41,14 @@
 
 
 def on_device(parcel_values, parcel_owner, parcel_cell, live_counts, fluid_state):
+
+    def launch_strings_all(local_x):
+        lower = lax.axis_size("gx")
+        state_next = jnp.split(local_x, lower, axis=1)
+        w_next = jnp.stack(state_next, axis=0)
+        a_now = lax.all_to_all(w_next, "gx", concat_axis=0, split_axis=0)
+        return jnp.concatenate(a_now, axis=2)
+
     channels, count_dev = parcel_values.shape
     width_x, width_y, width_z = (fluid_state.shape[1], fluid_state.shape[2], fluid_state.shape[3])
     owners = lax.axis_size("gx")
@@ -101,7 +109,7 @@
     smoothed = jnp.einsum(
         "ij,cjk->cik", banded(full_x, full_x, REACH), pencil, preferred_element_type=jnp.float32
     ).astype(jnp.bfloat16)
-    after_x = lax.all_to_all(smoothed, "gx", split_axis=1, concat_axis=2, tiled=True)
+    after_x = launch_strings_all(smoothed)
     after_x = after_x.reshape(channels, width_x, width_y, width_z)
     extended_y = padded(after_x, (("gy", 2),), REACH)
     after_y = jnp.einsum(

time: 158 us -> 152 us (0.962)
  blocking collectives: 27.7 us -> 22.1 us
    all_to_all x1, blocking collectives: 27.7 us -> 22.1 us  [launch_strings_all(): a_now = lax.all_to_all(w_next, 'gx', concat_axis=0, split_axis=0)]
where the time goes in v1:
time: 152 us; the launch traced here: 151 us
  waiting for transfers between devices  59.2 us (39%)
  local copies, waits for them, and re-layouts  37.1 us (24%)
  blocking collectives  22.1 us (15%)
  matrix products  12.6 us (8%)
  starting transfers between devices  12.5 us (8%)
  other arithmetic  6.6 us (4%)
    all_to_all x1, blocking collectives, launch_strings_all(): a_now = lax.all_to_all(w_next, 'gx', concat_axis=0, split_axis=0)  22.1 us
    ppermute x2, waiting for transfers between devices, padded(): before = lax.ppermute(last, axis, up)  19 us
    all_to_all x1, waiting for transfers between devices, on_device(): lax.all_to_all(flat_source, 'gx', split_axis=2, concat_axis=1, tiled=True)  18.1 us
    ppermute x2, waiting for transfers between devices, padded(): after = lax.ppermute(initial, axis, down)  14.6 us
    scatter x1, local copies, waits for them, and re-layouts, on_device(): packed = jnp.zeros((channels + 3, owners * capacity), jnp.bfloat16).at[:,...  11.4 us
    unnamed x8, local copies, waits for them, and re-layouts  9.98 us
    dot_general x6, matrix products, deposit(): jnp.einsum('sh,csz->chz', high_hot, weighted, preferred_element_type=jnp....  7.91 us
    all_to_all x1, waiting for transfers between devices, on_device(): lax.all_to_all(packed, 'gx', split_axis=1, concat_axis=1, tiled=True)  7.51 us
  transfers between devices with their start and end apart: 6, of which 6 were waited for; matrix products, arithmetic and copies ran while one was open for 1% of the time, Pallas kernels for 0%

profile of v1, /device:TPU:0, one launch (start us, length us, event | category | flops | bytes accessed | tf_op | source)
XLA Modules:
  0.0 151.2 jit_solution(13293237900098828716)
XLA Ops:
  0.7 0.7 fusion.61
  1.4 1.2 reduce-window.6
  2.6 0.2 slice_reduce_fusion
  2.8 0.2 reduce-window.9
  3.0 0.1 add_bitcast_fusion
  3.1 0.8 fusion.53
  3.9 0.8 fusion.79
  4.8 0.9 maximum_bitcast_fusion
  5.7 0.5 copy.24
  6.3 11.4 %scatter_custom_fusion = bf16[9,6144]{0,1:T(8,128)(2,1)S(1)} fusion(s32[4096]{0:T(1024)S(1)} %bitcast.91, bf16[4096,9]{1,0:T(8,128)(2,1)S(1)} %copy.24, bf16[]{:T(256)} %constant.117.clone.1), kind=kCustom, calls=%fused_computation.37 | custom fusion | bytes 110594 | tf_op jit(solution)/shard_map/scatter | solution.py:73
  17.6 1.4 copy.25
  19.0 6.3 %all-to-all-start = ((bf16[9,4,1536]{2,0,1:T(8,128)(2,1)}), bf16[9,4,1536]{2,0,1:T(8,128)(2,1)S(1)}, u32[]{:S(2)}, u32[]{:S(2)}) async-start(bf16[9,4,1536]{2,0,1:T(8,128)(2,1)} %copy.25), calls=%async_computation | async-start | bytes 393216 | tf_op jit(solution)/shard_map/all_to_all | solution.py:76
  25.3 7.5 %all-to-all-done = bf16[9,4,1536]{2,0,1:T(8,128)(2,1)S(1)} async-done(((bf16[9,4,1536]{2,0,1:T(8,128)(2,1)}), bf16[9,4,1536]{2,0,1:T(8,128)(2,1)S(1)}, u32[]{:S(2)}, u32[]{:S(2)}) %all-to-all-start) | async-done | bytes 110624 | tf_op jit(solution)/shard_map/all_to_all | solution.py:76
  32.8 0.1 copy.26
  33.1 9.3 %while.14 = (s32[]{:T(128)}, f32[6,512,128]{1,2,0:T(8,128)S(1)}, bf16[9,6144]{1,0:T(8,128)(2,1)S(1)}, s32[]{:T(128)}, s32[]{:T(128)}, /*index=5*/s32[]{}, s32[]{:T(128)}, s32[]{:T(128)}, s32[]{}, s32[]{}) while((s32[]{:T(128)}, f32[6,512,128]{1,2,0:T(8,128)S(1)}, bf16[9,6144]{1,0:T(8,128)(2,1)S(1)}, s32[]{:T(128)}, s32[]{:T(128)}, ...), condition=%wide.region_5.6_spmd.clone, body=%wide.region_4.5_spmd.clone.sunk | while | flops 807670784 | bytes 3729625 | solution.py:99
  33.1 0.1 fusion.132
  33.2 0.1 fusion.131
  33.3 1.3 bitcast_add_fusion.2
  34.6 0.1 fusion.132
  34.7 0.1 fusion.131
  34.8 1.3 bitcast_add_fusion.2
  36.2 0.1 fusion.132
  36.3 0.1 fusion.131
  36.4 1.3 bitcast_add_fusion.2
  37.7 0.1 fusion.132
  37.8 0.1 fusion.131
  37.9 1.3 bitcast_add_fusion.2
  39.3 0.1 fusion.132
  39.4 0.1 fusion.131
  39.5 1.3 bitcast_add_fusion.2
  40.8 0.1 fusion.132
  40.9 0.1 fusion.131
  41.0 1.3 bitcast_add_fusion.2
  42.4 0.1 convert_element_type.119
  42.5 0.4 copy.27
  42.8 0.3 convert_element_type.120
  43.2 4.2 %copy.28 = bf16[6,32,2048]{1,0,2:T(8,128)(2,1)} copy(bf16[6,32,2048]{2,1,0:T(8,128)(2,1)S(1)} %convert_element_type.120) | data formatting | bytes 1572864 | tf_op jit(solution)/shard_map/convert_element_type | solution.py:105
  47.4 5.7 %reshape.137 = bf16[4,2,49152]{2,1,0:T(2,128)(2,1)} reshape(bf16[2048,6,32]{2,1,0:T(8,128)(2,1)} %bitcast.78) | data formatting | bytes 1572864
  53.1 3.5 %all-to-all-start.1 = ((bf16[4,2,49152]{2,1,0:T(2,128)(2,1)}), bf16[4,2,49152]{2,1,0:T(2,128)(2,1)S(1)}, u32[]{:S(2)}, u32[]{:S(2)}) async-start(bf16[4,2,49152]{2,1,0:T(2,128)(2,1)} %reshape.137), calls=%async_computation.1 | async-start | bytes 1572864 | tf_op jit(solution)/shard_map/all_to_all | solution.py:107
  56.6 0.6 fusion.104
  57.2 18.1 %all-to-all-done.1 = bf16[4,2,49152]{2,1,0:T(2,128)(2,1)S(1)} async-done(((bf16[4,2,49152]{2,1,0:T(2,128)(2,1)}), bf16[4,2,49152]{2,1,0:T(2,128)(2,1)S(1)}, u32[]{:S(2)}, u32[]{:S(2)}) %all-to-all-start.1) | async-done | bytes 786464 | tf_op jit(solution)/shard_map/all_to_all | solution.py:107
  75.3 4.2 %reshape.138 = bf16[2048,6,32]{2,1,0:T(8,128)(2,1)} reshape(bf16[4,2,49152]{2,1,0:T(2,128)(2,1)S(1)} %all-to-all-done.1) | data formatting | bytes 1572864
  79.5 4.5 %copy.38 = bf16[6,32,4,512]{3,2,1,0:T(4,128)(2,1)S(1)} copy(bf16[6,32,4,512]{1,0,3,2:T(8,128)(2,1)} %bitcast.79) | data formatting | bytes 1572864 | tf_op jit(solution)/shard_map/all_to_all | solution.py:107
  84.0 0.2 copy.30
  84.2 1.0 fusion.38
  85.1 0.1 slice_bitcast_fusion.3
  85.2 0.1 pad_maximum_fusion
  85.3 22.1 %all_to_all.28 = bf16[4,6,32,512]{3,2,1,0:T(8,128)(2,1)S(1)} all-to-all(bf16[4,6,32,512]{3,2,1,0:T(8,128)(2,1)S(1)} %pad_maximum_fusion), channel_id=1, replica_groups=mesh['grp'=2,'gx'=4,'gy'=2,'gz'=2] {'gx'}, dimensions={0} | all-to-all | bytes 1572864 | tf_op jit(solution)/shard_map/all_to_all | solution.py:49
  107.4 0.6 copy.31
  108.0 0.3 reshape_reshape.3
  108.3 1.6 %collective-permute-start = (bf16[6,32,16,128]{3,2,1,0:T(8,128)(2,1)S(1)}, bf16[6,32,16,128]{3,2,1,0:T(8,128)(2,1)S(1)}, u32[]{:S(2)}, u32[]{:S(2)}) collective-permute-start(bf16[6,32,16,128]{3,2,1,0:T(8,128)(2,1)S(1)} %reshape_reshape.3), channel_id=1, source_target_pairs={{0,2},{2,0},{1,3},{3,1},{4,6},{6,4},{5,7},{7,5},{8,10},{10,8},{9,1... | collective-permute-start | bytes 2359304 | tf_op jit(solution)/shard_map/ppermute | solution.py:17
  109.9 0.5 collective-permute-start.1
  110.4 18.5 %collective-permute-done = bf16[6,32,16,128]{3,2,1,0:T(8,128)(2,1)S(1)} collective-permute-done((bf16[6,32,16,128]{3,2,1,0:T(8,128)(2,1)S(1)}, bf16[6,32,16,128]{3,2,1,0:T(8,128)(2,1)S(1)}, u32[]{:S(2)}, u32[]{:S(2)}) %collective-permute-start) | collective-permute-done | bytes 786464 | tf_op jit(solution)/shard_map/ppermute | solution.py:17
  128.8 14.4 %collective-permute-done.1 = bf16[6,32,16,128]{3,2,1,0:T(8,128)(2,1)S(1)} collective-permute-done((bf16[6,32,16,128]{3,2,1,0:T(8,128)(2,1)S(1)}, bf16[6,32,16,128]{3,2,1,0:T(8,128)(2,1)S(1)}, u32[]{:S(2)}, u32[]{:S(2)}) %collective-permute-start.1) | collective-permute-done | bytes 786464 | tf_op jit(solution)/shard_map/ppermute | solution.py:18
  143.3 1.1 fusion.35
  144.4 0.4 fusion.123
  144.7 0.6 copy.32
  145.5 0.6 copy.33
  146.1 0.5 collective-permute-start.3
  146.6 0.5 collective-permute-done.2
  147.1 0.6 copy.34
  147.8 0.2 collective-permute-done.3
  148.0 0.6 copy.35
  148.6 2.6 %add_convert_fusion = bf16[6,32,16,128]{3,2,1,0:T(8,128)(2,1)} fusion(bf16[6,32,16,128]{3,2,1,0:T(8,128)(2,1)S(1)} %copy-done.1, bf16[6,32,16,16]{3,2,1,0:T(8,128)(2,1)S(1)} %copy.35, bf16[6,32,16,128]{3,2,1,0:T(8,128)(2,1)S(1)} %fusion.35, bf16[6,32,16,16]{3,2,1,0:T(8,128)(2,1)S(1)} %copy.34, f32[]{:T(128)} %fusion.104), kind=kOutput, calls=%fused_computation.31 | convolution fusion | flops 130203648 | bytes 2555908 | tf_op jit(solution)/shard_map/cxyj,ij->cxyi/dot_general | solution.py:122
  (27 shorter events, 0.4 us)
Async XLA Ops:
  0.0 6.2 %copy-start = (s32[4096,1]{0,1:T(1,128)S(1)}, s32[4096,1]{0,1:T(1,128)}, u32[]{:S(2)}) copy-start(s32[4096,1]{0,1:T(1,128)} %param.8) | copy-start | bytes 49156
  19.0 13.8 %all-to-all-start = ((bf16[9,4,1536]{2,0,1:T(8,128)(2,1)}), bf16[9,4,1536]{2,0,1:T(8,128)(2,1)S(1)}, u32[]{:S(2)}, u32[]{:S(2)}) async-start(bf16[9,4,1536]{2,0,1:T(8,128)(2,1)} %copy.25), calls=%async_computation | async-start | bytes 393216 | tf_op jit(solution)/shard_map/all_to_all | solution.py:76
  53.1 22.2 %all-to-all-start.1 = ((bf16[4,2,49152]{2,1,0:T(2,128)(2,1)}), bf16[4,2,49152]{2,1,0:T(2,128)(2,1)S(1)}, u32[]{:S(2)}, u32[]{:S(2)}) async-start(bf16[4,2,49152]{2,1,0:T(2,128)(2,1)} %reshape.137), calls=%async_computation.1 | async-start | bytes 1572864 | tf_op jit(solution)/shard_map/all_to_all | solution.py:107
  108.3 20.5 %collective-permute-start = (bf16[6,32,16,128]{3,2,1,0:T(8,128)(2,1)S(1)}, bf16[6,32,16,128]{3,2,1,0:T(8,128)(2,1)S(1)}, u32[]{:S(2)}, u32[]{:S(2)}) collective-permute-start(bf16[6,32,16,128]{3,2,1,0:T(8,128)(2,1)S(1)} %reshape_reshape.3), channel_id=1, source_target_pairs={{0,2},{2,0},{1,3},{3,1},{4,6},{6,4},{5,7},{7,5},{8,10},{10,8},{9,1... | collective-permute-start | bytes 2359304 | tf_op jit(solution)/shard_map/ppermute | solution.py:17
  109.9 33.4 %collective-permute-start.1 = (bf16[6,32,16,128]{3,2,1,0:T(8,128)(2,1)S(1)}, bf16[6,32,16,128]{3,2,1,0:T(8,128)(2,1)S(1)}, u32[]{:S(2)}, u32[]{:S(2)}) collective-permute-start(bf16[6,32,16,128]{3,2,1,0:T(8,128)(2,1)S(1)} %reshape_reshape.3), channel_id=1, source_target_pairs={{2,0},{0,2},{3,1},{1,3},{6,4},{4,6},{7,5},{5,7},{10,8},{8,10},{11,... | collective-permute-start | bytes 2359304 | tf_op jit(solution)/shard_map/ppermute | solution.py:18
  145.4 1.8 %collective-permute-start.2 = (bf16[6,32,16,16]{1,3,2,0:T(8,128)(2,1)S(1)}, bf16[6,32,16,16]{1,3,2,0:T(8,128)(2,1)S(1)}, u32[]{:S(2)}, u32[]{:S(2)}) collective-permute-start(bf16[6,32,16,16]{1,3,2,0:T(8,128)(2,1)S(1)} %copy.32), channel_id=1, source_target_pairs={{0,1},{1,0},{2,3},{3,2},{4,5},{5,4},{6,7},{7,6},{8,9},{9,8},{10,11... | collective-permute-start | bytes 294920 | tf_op jit(solution)/shard_map/ppermute | solution.py:17
  145.4 3.2 %copy-start.1 = (bf16[6,32,16,128]{3,2,1,0:T(8,128)(2,1)S(1)}, bf16[6,32,16,128]{3,2,1,0:T(8,128)(2,1)}, u32[]{:S(2)}) copy-start(bf16[6,32,16,128]{3,2,1,0:T(8,128)(2,1)} %param.11) | copy-start | bytes 2359300
  146.1 1.9 %collective-permute-start.3 = (bf16[6,32,16,16]{1,3,2,0:T(8,128)(2,1)S(1)}, bf16[6,32,16,16]{1,3,2,0:T(8,128)(2,1)S(1)}, u32[]{:S(2)}, u32[]{:S(2)}) collective-permute-start(bf16[6,32,16,16]{1,3,2,0:T(8,128)(2,1)S(1)} %copy.33), channel_id=1, source_target_pairs={{1,0},{0,1},{3,2},{2,3},{5,4},{4,5},{7,6},{6,7},{9,8},{8,9},{11,10... | collective-permute-start | bytes 294920 | tf_op jit(solution)/shard_map/ppermute | solution.py:18
